TPU v7x, 256 devices: a whole 4x4x8 slice. The times are simulated.
256 devices in a mesh: row: 16 (over y, x), col: 16 (over z, core).
Axes of the slice: x: 4, y: 4, z: 8, core: 2. Of those that a mesh axis runs over, the one named last changes fastest.
Arguments:
- matrix: bfloat16 [24576, 24576], P('row', 'col'), may hold values from -6 to 6
- inverses: bfloat16 [2, 256, 256], replicated, may hold values from -0.09 to 0.1, as said below
Outputs:
- factored: bfloat16 [24576, 24576], P('row', 'col')
- panels: bfloat16 [24576, 512], P('row')
Inputs may be any that keep to these rules, and one draw needn't show every extreme that they name: `inverses`: each of the two matrices is lower triangular with a diagonal between 0.05 and 0.1.
All inputs are finite; a program needn't handle non-finite values.
Results may differ from a plain program's by a relative error of at most 0.0057.
Values may be sent and summed in bfloat16 or wider, within the bound.
No kernel may reach another device: no remote copies, remote signals or barrier semaphores. Data moves between devices by JAX's collectives and lax.ppermute only.
A program may use at most 128 MiB of HBM per device.

v0:
```python
import jax
import jax.numpy as jnp
from jax import lax
from jax.sharding import PartitionSpec as P


def from_root(value, axis, source):
    kept = jnp.where(lax.axis_index(axis) == source, value, 0).astype(value.dtype)
    return lax.psum(kept, axis)


def outer_term(left_rows, right_rows):
    return lax.dot_general(
        left_rows, right_rows, (((1,), (1,)), ((), ())), preferred_element_type=jnp.float32
    )


def shards(matrix, inverses):
    width = inverses.shape[1]
    rows_local = matrix.shape[0]
    row_count = lax.axis_size("row")
    col_count = lax.axis_size("col")
    row_rank = lax.axis_index("row")
    col_rank = lax.axis_index("col")
    blocks_row = rows_local // width
    blocks_col = matrix.shape[1] // width
    ratio_blocks = col_count // row_count
    global_rows = jnp.repeat(jnp.arange(blocks_row, dtype=jnp.int32) * row_count + row_rank, width)
    source_row = col_rank % row_count
    source_slot = col_rank // row_count

    def factor(panel, inverse, start_block, owner_col):
        product = jnp.dot(panel, inverse.T, preferred_element_type=jnp.float32)
        masked = jnp.where((global_rows >= start_block)[:, None], product, 0.0).astype(jnp.bfloat16)
        return from_root(masked, "col", owner_col)

    def columns_of(left_rows):
        gathered = lax.all_gather(left_rows, "row", axis=0, tiled=True)
        gathered = gathered.reshape(row_count, blocks_col, ratio_blocks, width, width)
        mine = lax.dynamic_index_in_dim(gathered, source_row, 0, keepdims=False)
        mine = lax.dynamic_index_in_dim(mine, source_slot, 1, keepdims=False)
        return mine.reshape(blocks_col * width, width)

    first_rows = factor(matrix[:, :width], inverses[0], 1, 0)
    first_cols = columns_of(first_rows)
    partial_value = matrix.astype(jnp.float32) - outer_term(first_rows, first_cols)
    head = partial_value[:, :width].astype(jnp.bfloat16)
    second_rows = factor(head, inverses[1], 2, 1)
    second_cols = columns_of(second_rows)
    factored = (partial_value - outer_term(second_rows, second_cols)).astype(jnp.bfloat16)
    return (factored, jnp.concatenate([first_rows, second_rows], axis=1))


def solution(mesh):
    return jax.shard_map(
        shards,
        mesh=mesh,
        in_specs=(P("row", "col"), P()),
        out_specs=(P("row", "col"), P("row", None)),
        check_vma=False,
    )
```

profile of v0, /device:TPU:1, one launch (start us, length us, event | category | flops | bytes accessed | tf_op | source)
XLA Modules:
  0.0 456.7 jit_solution(4977230878266750554)
XLA Ops:
  7.2 0.0 all-reduce.3.cloned.1.call-start
  7.2 0.1 broadcast_in_dim.30
  7.3 2.5 fusion.4
  9.8 0.0 all-reduce.3.cloned.1.call-update
  9.8 0.0 all-gather.3.cloned.1.call-start
  9.9 115.4 %all-reduce.3.cloned.1.call-done = bf16[1536,256]{1,0:T(8,128)(2,1)} async-done(((bf16[1536,256]{1,0:T(8,128)(2,1)}), bf16[1536,256]{1,0:T(8,128)(2,1)}) %all-reduce.3.cloned.1.call-update) | async-done | bytes 786448 | tf_op jit(solution)/shard_map/psum | solution.py:9
  125.2 0.0 all-gather.3.cloned.1.call-update
  125.3 0.0 all-reduce.5.cloned.1.call-start
  125.3 0.1 broadcast_in_dim.34
  125.4 98.0 %all-gather.3.cloned.1.call-done = bf16[24576,256]{1,0:T(8,128)(2,1)} async-done(((bf16[1536,256]{1,0:T(8,128)(2,1)}), bf16[24576,256]{1,0:T(8,128)(2,1)}) %all-gather.3.cloned.1.call-update) | async-done | bytes 12582928 | tf_op jit(solution)/shard_map/all_gather | solution.py:38
  223.4 1.2 constant_dynamic-slice_fusion.1
  224.6 0.0 copy-start.3
  224.6 4.0 convolution_subtract_fusion.1
  228.6 0.0 copy-start
  228.7 3.5 copy-done
  232.2 0.0 copy-done.3
  232.2 0.0 copy-start.1
  232.2 1.3 fusion.3
  233.5 0.0 all-reduce.5.cloned.1.call-update
  233.5 0.0 all-gather.5.cloned.1.call-start
  233.6 110.4 %all-reduce.5.cloned.1.call-done = bf16[1536,256]{1,0:T(8,128)(2,1)} async-done(((bf16[1536,256]{1,0:T(8,128)(2,1)}), bf16[1536,256]{1,0:T(8,128)(2,1)}) %all-reduce.5.cloned.1.call-update) | async-done | bytes 786448 | tf_op jit(solution)/shard_map/psum | solution.py:9
  343.9 0.0 copy-start.2
  343.9 0.0 all-gather.5.cloned.1.call-update
  343.9 0.0 copy-done.1
  344.0 2.5 pad_maximum_fusion
  346.4 95.2 %all-gather.5.cloned.1.call-done = bf16[24576,256]{1,0:T(8,128)(2,1)} async-done(((bf16[1536,256]{1,0:T(8,128)(2,1)}), bf16[24576,256]{1,0:T(8,128)(2,1)}) %all-gather.5.cloned.1.call-update) | async-done | bytes 12582928 | tf_op jit(solution)/shard_map/all_gather | solution.py:38
  441.6 1.2 constant_dynamic-slice_fusion
  442.8 0.0 copy-done.2
  442.8 7.3 %fusion = bf16[1536,1536]{1,0:T(8,128)(2,1)} fusion(f32[1536,1536]{1,0:T(8,128)} %copy-done, bf16[1536,256]{1,0:T(8,128)(2,1)S(1)} %copy-done.2, bf16[1536,256]{1,0:T(8,128)(2,1)S(1)} %bitcast.15), kind=kOutput, calls=%fused_computation.2 | convolution fusion | flops 1212678144 | bytes 15728640 | tf_op jit(solution)/shard_map/dot_general | solution.py:13
  (3 shorter events, 0.0 us)
Async XLA Ops:
  7.2 118.1 %all-reduce.3.cloned.1.call-start = ((), (), s32[]{:S(2)}) async-start(), calls=%async_computation | async-start | bytes 1572864 | tf_op jit(solution)/shard_map/psum | solution.py:9
  9.8 213.6 %all-gather.3.cloned.1.call-start = ((), (), s32[]{:S(2)}) async-start(), calls=%async_computation.1 | async-start | bytes 13369344 | tf_op jit(solution)/shard_map/all_gather | solution.py:38
  125.3 218.7 %all-reduce.5.cloned.1.call-start = ((), (), s32[]{:S(2)}) async-start(), calls=%async_computation.2 | async-start | bytes 1572864 | tf_op jit(solution)/shard_map/psum | solution.py:9
  224.6 7.6 %copy-start.3 = (bf16[2,256,256]{2,1,0:T(8,128)(2,1)S(1)}, bf16[2,256,256]{2,1,0:T(8,128)(2,1)}, u32[]{:S(2)}) copy-start(bf16[2,256,256]{2,1,0:T(8,128)(2,1)} %param.3) | copy-start | bytes 786436
  228.6 3.5 copy-start
  232.2 111.8 %copy-start.1 = (bf16[1536,256]{1,0:T(8,128)(2,1)S(1)}, bf16[1536,256]{1,0:T(8,128)(2,1)}, u32[]{:S(2)}) copy-start(bf16[1536,256]{1,0:T(8,128)(2,1)} %all-reduce.3.cloned.1.call-done) | copy-start | bytes 2359300
  233.5 208.1 %all-gather.5.cloned.1.call-start = ((), (), s32[]{:S(2)}) async-start(), calls=%async_computation.3 | async-start | bytes 13369344 | tf_op jit(solution)/shard_map/all_gather | solution.py:38
  343.9 98.9 %copy-start.2 = (bf16[1536,256]{1,0:T(8,128)(2,1)S(1)}, bf16[1536,256]{1,0:T(8,128)(2,1)}, u32[]{:S(2)}) copy-start(bf16[1536,256]{1,0:T(8,128)(2,1)} %all-reduce.5.cloned.1.call-done) | copy-start | bytes 2359300
Sparse Core Ops, SparseCore 0:
  10.9 114.2 all-reduce.2
  128.0 95.3 all-gather.2
  233.6 110.2 all-reduce.4
  346.2 95.3 all-gather.4
where the time goes:
time: 457 us
  waiting for transfers between devices  419 us (92%)
  matrix products  15.1 us (3%)
  between operations  13.8 us (3%)
  local copies, waits for them, and re-layouts  6.09 us (1%)
    psum x2, waiting for transfers between devices, from_root(): return lax.psum(kept, axis)  226 us
    all_gather x2, waiting for transfers between devices, columns_of(): gathered = lax.all_gather(left_rows, 'row', axis=0, tiled=True)  193 us
    dot_general x2, matrix products, outer_term(): lax.dot_general(left_rows, right_rows, (((1,), (1,)), ((), ())), preferre...  11.3 us
  transfers between devices with their start and end apart: 4, of which 4 were waited for; matrix products, arithmetic and copies ran while one was open for 1% of the time, Pallas kernels for 0%

commit v1 on v0

--- a/solution.py
+++ b/solution.py
@@ -6,7 +6,7 @@
 
 def from_root(value, axis, source):
     kept = jnp.where(lax.axis_index(axis) == source, value, 0).astype(value.dtype)
-    return lax.psum(kept, axis)
+    return jnp.sum(lax.all_gather(kept, axis), axis=0)
 
 
 def outer_term(left_rows, right_rows):

time: 457 us -> 393 us (0.86)
  waiting for transfers between devices: 419 us -> 340 us
  other arithmetic: 2.46 us -> 17.4 us
    psum x2 -> x0, waiting for transfers between devices: 226 us -> none  [from_root(): return lax.psum(kept, axis)]
    all_gather x0 -> x2, waiting for transfers between devices: none -> 156 us  [from_root(): return jnp.sum(lax.all_gather(kept, axis), axis=0)]
    reduce_sum x0 -> x2, other arithmetic: none -> 14.9 us  [from_root(): return jnp.sum(lax.all_gather(kept, axis), axis=0)]
    all_gather x2, waiting for transfers between devices: 193 us -> 184 us  [columns_of(): gathered = lax.all_gather(left_rows, 'row', axis=0, tiled=True)]
where the time goes in v1:
time: 393 us
  waiting for transfers between devices  340 us (87%)
  other arithmetic  17.4 us (4%)
  matrix products  15.1 us (4%)
  between operations  13.8 us (4%)
  local copies, waits for them, and re-layouts  6.09 us (2%)
    all_gather x2, waiting for transfers between devices, columns_of(): gathered = lax.all_gather(left_rows, 'row', axis=0, tiled=True)  184 us
    all_gather x2, waiting for transfers between devices, from_root(): return jnp.sum(lax.all_gather(kept, axis), axis=0)  156 us
    reduce_sum x2, other arithmetic, from_root(): return jnp.sum(lax.all_gather(kept, axis), axis=0)  14.9 us
    dot_general x2, matrix products, outer_term(): lax.dot_general(left_rows, right_rows, (((1,), (1,)), ((), ())), preferre...  11.3 us
  transfers between devices with their start and end apart: 4, of which 4 were waited for; matrix products, arithmetic and copies ran while one was open for 1% of the time, Pallas kernels for 0%

profile of v1, /device:TPU:1, one launch (start us, length us, event | category | flops | bytes accessed | tf_op | source)
XLA Modules:
  0.0 393.0 jit_solution(13717554364815691284)
XLA Ops:
  7.2 0.0 all-gather.11.cloned.1.call-start
  7.2 0.1 broadcast_in_dim.30
  7.3 2.5 fusion.4
  9.8 0.0 all-gather.11.cloned.1.call-update
  9.8 0.0 all-gather.7.cloned.1.call-start
  9.9 80.5 %all-gather.11.cloned.1.call-done = bf16[24576,256]{1,0:T(8,128)(2,1)} async-done(((bf16[1536,256]{1,0:T(8,128)(2,1)}), bf16[24576,256]{1,0:T(8,128)(2,1)}) %all-gather.11.cloned.1.call-update) | async-done | bytes 12582928 | tf_op jit(solution)/shard_map/all_gather | solution.py:9
  90.3 7.4 %reduce_sum.24 = bf16[1536,256]{1,0:T(8,128)(2,1)} reduce(bf16[16,1536,256]{2,1,0:T(8,128)(2,1)} %bitcast.17, bf16[]{:T(256)} %constant.50.clone.1), dimensions={0}, to_apply=%region_0.1 | reduce | flops 5898240 | bytes 13369346 | tf_op jit(solution)/shard_map/reduce_sum | solution.py:9
  97.8 0.0 all-gather.7.cloned.1.call-update
  97.8 0.0 all-gather.13.cloned.1.call-start
  97.8 0.1 broadcast_in_dim.34
  97.9 93.1 %all-gather.7.cloned.1.call-done = bf16[24576,256]{1,0:T(8,128)(2,1)} async-done(((bf16[1536,256]{1,0:T(8,128)(2,1)}), bf16[24576,256]{1,0:T(8,128)(2,1)}) %all-gather.7.cloned.1.call-update) | async-done | bytes 12582928 | tf_op jit(solution)/shard_map/all_gather | solution.py:38
  191.1 1.2 constant_dynamic-slice_fusion.1
  192.3 0.0 copy-start.3
  192.3 4.0 %convolution_subtract_fusion.1 = f32[1536,1536]{1,0:T(8,128)S(1)} fusion(bf16[1536,256]{1,0:T(8,128)(2,1)} %reduce_sum.24, bf16[1536,256]{1,0:T(8,128)(2,1)S(1)} %bitcast.18, bf16[1536,1536]{1,0:T(8,128)(2,1)} %param.2), kind=kOutput, calls=%fused_computation.1 | convolution fusion | flops 1212678144 | bytes 15728640 | tf_op jit(solution)/shard_map/dot_general | solution.py:13
  196.3 0.0 copy-start
  196.3 3.5 copy-done
  199.9 0.0 copy-done.3
  199.9 1.3 fusion.3
  201.2 0.0 all-gather.13.cloned.1.call-update
  201.2 0.0 all-gather.9.cloned.1.call-start
  201.2 75.9 %all-gather.13.cloned.1.call-done = bf16[24576,256]{1,0:T(8,128)(2,1)} async-done(((bf16[1536,256]{1,0:T(8,128)(2,1)}), bf16[24576,256]{1,0:T(8,128)(2,1)}) %all-gather.13.cloned.1.call-update) | async-done | bytes 12582928 | tf_op jit(solution)/shard_map/all_gather | solution.py:9
  277.2 0.0 copy-start.1
  277.2 7.5 %reduce_sum.25 = bf16[1536,256]{1,0:T(8,128)(2,1)} reduce(bf16[16,1536,256]{2,1,0:T(8,128)(2,1)} %bitcast.16, bf16[]{:T(256)} %constant.50.clone.1), dimensions={0}, to_apply=%region_1.2 | reduce | flops 5898240 | bytes 13369346 | tf_op jit(solution)/shard_map/reduce_sum | solution.py:9
  284.7 0.0 copy-start.2
  284.7 0.0 all-gather.9.cloned.1.call-update
  284.7 0.0 copy-done.1
  284.7 2.5 pad_maximum_fusion
  287.2 90.8 %all-gather.9.cloned.1.call-done = bf16[24576,256]{1,0:T(8,128)(2,1)} async-done(((bf16[1536,256]{1,0:T(8,128)(2,1)}), bf16[24576,256]{1,0:T(8,128)(2,1)}) %all-gather.9.cloned.1.call-update) | async-done | bytes 12582928 | tf_op jit(solution)/shard_map/all_gather | solution.py:38
  378.0 1.2 constant_dynamic-slice_fusion
  379.2 0.0 copy-done.2
  379.2 7.3 %fusion = bf16[1536,1536]{1,0:T(8,128)(2,1)} fusion(f32[1536,1536]{1,0:T(8,128)} %copy-done, bf16[1536,256]{1,0:T(8,128)(2,1)S(1)} %copy-done.2, bf16[1536,256]{1,0:T(8,128)(2,1)S(1)} %bitcast.19), kind=kOutput, calls=%fused_computation.2 | convolution fusion | flops 1212678144 | bytes 15728640 | tf_op jit(solution)/shard_map/dot_general | solution.py:13
  (3 shorter events, 0.0 us)
Async XLA Ops:
  7.2 83.2 %all-gather.11.cloned.1.call-start = ((), (), s32[]{:S(2)}) async-start(), calls=%async_computation.2 | async-start | bytes 13369344 | tf_op jit(solution)/shard_map/all_gather | solution.py:9
  9.8 181.3 %all-gather.7.cloned.1.call-start = ((), (), s32[]{:S(2)}) async-start(), calls=%async_computation | async-start | bytes 13369344 | tf_op jit(solution)/shard_map/all_gather | solution.py:38
  97.8 179.4 %all-gather.13.cloned.1.call-start = ((), (), s32[]{:S(2)}) async-start(), calls=%async_computation.3 | async-start | bytes 13369344 | tf_op jit(solution)/shard_map/all_gather | solution.py:9
  192.3 7.6 %copy-start.3 = (bf16[2,256,256]{2,1,0:T(8,128)(2,1)S(1)}, bf16[2,256,256]{2,1,0:T(8,128)(2,1)}, u32[]{:S(2)}) copy-start(bf16[2,256,256]{2,1,0:T(8,128)(2,1)} %param.3) | copy-start | bytes 786436
  196.3 3.5 copy-start
  201.2 176.8 %all-gather.9.cloned.1.call-start = ((), (), s32[]{:S(2)}) async-start(), calls=%async_computation.1 | async-start | bytes 13369344 | tf_op jit(solution)/shard_map/all_gather | solution.py:38
  277.2 7.5 %copy-start.1 = (bf16[1536,256]{1,0:T(8,128)(2,1)S(1)}, bf16[1536,256]{1,0:T(8,128)(2,1)}, u32[]{:S(2)}) copy-start(bf16[1536,256]{1,0:T(8,128)(2,1)} %reduce_sum.24) | copy-start | bytes 2359300
  284.7 94.5 %copy-start.2 = (bf16[1536,256]{1,0:T(8,128)(2,1)S(1)}, bf16[1536,256]{1,0:T(8,128)(2,1)}, u32[]{:S(2)}) copy-start(bf16[1536,256]{1,0:T(8,128)(2,1)} %reduce_sum.25) | copy-start | bytes 2359300
Sparse Core Ops, SparseCore 0:
  10.4 79.8 all-gather.10
  97.9 93.1 all-gather.6
  201.3 75.8 all-gather.12
  284.8 93.1 all-gather.8

commit v2 on v0

--- a/solution.py
+++ b/solution.py
@@ -35,7 +35,9 @@
         return from_root(masked, "col", owner_col)
 
     def columns_of(left_rows):
-        gathered = lax.all_gather(left_rows, "row", axis=0, tiled=True)
+        gathered = jnp.concatenate(
+            lax.all_to_all(jnp.stack([left_rows] * lax.axis_size("row")), "row", 0, 0), axis=0
+        )
         gathered = gathered.reshape(row_count, blocks_col, ratio_blocks, width, width)
         mine = lax.dynamic_index_in_dim(gathered, source_row, 0, keepdims=False)
         mine = lax.dynamic_index_in_dim(mine, source_slot, 1, keepdims=False)

time: 457 us -> 665 us (1.46)
  waiting for transfers between devices: 419 us -> 596 us
  local copies, waits for them, and re-layouts: 6.09 us -> 19.8 us
  starting transfers between devices: 0.16 us -> 13.5 us
    all_to_all x0 -> x2, waiting for transfers between devices: none -> 369 us  [columns_of(): lax.all_to_all(jnp.stack([left_rows] * lax.axis_size('row')), 'row', 0, 0)]
    all_gather x2 -> x0, waiting for transfers between devices: 193 us -> none  [columns_of(): gathered = lax.all_gather(left_rows, 'row', axis=0, tiled=True)]
    another operation x0 -> x2, local copies, waits for them, and re-layouts: none -> 13.6 us  [columns_of(): jnp.stack([left_rows] * lax.axis_size('row'))]
    all_to_all x0 -> x2, starting transfers between devices: none -> 13.4 us  [columns_of(): lax.all_to_all(jnp.stack([left_rows] * lax.axis_size('row')), 'row', 0, 0)]
  transfers between devices with their start and end apart: 4 -> 4, of which waited for: 4 -> 4; matrix products, arithmetic and copies ran while one was open for 1% -> 0% of each run, Pallas kernels for 0% -> 0%
where the time goes in v2:
time: 665 us; the launch traced here: 660 us
  waiting for transfers between devices  596 us (90%)
  local copies, waits for them, and re-layouts  19.8 us (3%)
  matrix products  14.9 us (2%)
  between operations  14.1 us (2%)
  starting transfers between devices  13.5 us (2%)
    all_to_all x2, waiting for transfers between devices, columns_of(): lax.all_to_all(jnp.stack([left_rows] * lax.axis_size('row')), 'row', 0, 0)  369 us
    psum x2, waiting for transfers between devices, from_root(): return lax.psum(kept, axis)  227 us
    another operation x2, local copies, waits for them, and re-layouts, columns_of(): jnp.stack([left_rows] * lax.axis_size('row'))  13.6 us
    all_to_all x2, starting transfers between devices, columns_of(): lax.all_to_all(jnp.stack([left_rows] * lax.axis_size('row')), 'row', 0, 0)  13.4 us
  transfers between devices with their start and end apart: 4, of which 4 were waited for; matrix products, arithmetic and copies ran while one was open for 0% of the time, Pallas kernels for 0%

profile of v2, /device:TPU:1, one launch (start us, length us, event | category | flops | bytes accessed | tf_op | source)
XLA Modules:
  0.0 659.8 jit_solution(13167815841436633145)
XLA Ops:
  7.2 0.0 all-reduce.3.cloned.1.call-start
  7.2 0.1 broadcast_in_dim.30
  7.3 2.5 fusion.4
  9.8 0.0 all-reduce.3.cloned.1.call-update
  9.8 115.4 %all-reduce.3.cloned.1.call-done = bf16[1536,256]{1,0:T(8,128)(2,1)} async-done(((bf16[1536,256]{1,0:T(8,128)(2,1)}), bf16[1536,256]{1,0:T(8,128)(2,1)}) %all-reduce.3.cloned.1.call-update) | async-done | bytes 786448 | tf_op jit(solution)/shard_map/psum | solution.py:9
  125.2 6.8 %stack.4 = bf16[16,1536,256]{2,1,0:T(8,128)(2,1)} broadcast(bf16[1536,256]{1,0:T(8,128)(2,1)} %all-reduce.3.cloned.1.call-done), dimensions={1,2} | broadcast | bytes 13369344 | tf_op jit(solution)/shard_map/stack | solution.py:39
  132.1 0.0 copy-start.1
  132.1 6.7 %all-to-all-start = ((bf16[16,1536,256]{2,1,0:T(8,128)(2,1)}), bf16[16,1536,256]{2,1,0:T(8,128)(2,1)}, u32[]{:S(2)}, u32[]{:S(2)}) async-start(bf16[16,1536,256]{2,1,0:T(8,128)(2,1)} %stack.4), calls=%async_computation | async-start | bytes 25165824 | tf_op jit(solution)/shard_map/all_to_all | solution.py:39
  138.8 0.0 all-reduce.5.cloned.1.call-start
  138.8 0.1 broadcast_in_dim.34
  138.9 185.2 %all-to-all-done = bf16[16,1536,256]{2,1,0:T(8,128)(2,1)} async-done(((bf16[16,1536,256]{2,1,0:T(8,128)(2,1)}), bf16[16,1536,256]{2,1,0:T(8,128)(2,1)}, u32[]{:S(2)}, u32[]{:S(2)}) %all-to-all-start) | async-done | bytes 12582944 | tf_op jit(solution)/shard_map/all_to_all | solution.py:39
  324.1 1.2 constant_dynamic-slice_fusion.1
  325.3 0.0 copy-done.1
  325.3 0.0 copy-start.3
  325.3 3.8 convolution_subtract_fusion.1
  329.1 0.0 copy-start
  329.1 3.6 copy-done
  332.7 0.0 copy-done.3
  332.7 1.3 fusion.3
  334.0 0.0 all-reduce.5.cloned.1.call-update
  334.0 111.6 %all-reduce.5.cloned.1.call-done = bf16[1536,256]{1,0:T(8,128)(2,1)} async-done(((bf16[1536,256]{1,0:T(8,128)(2,1)}), bf16[1536,256]{1,0:T(8,128)(2,1)}) %all-reduce.5.cloned.1.call-update) | async-done | bytes 786448 | tf_op jit(solution)/shard_map/psum | solution.py:9
  445.6 6.8 %stack.5 = bf16[16,1536,256]{2,1,0:T(8,128)(2,1)} broadcast(bf16[1536,256]{1,0:T(8,128)(2,1)} %all-reduce.5.cloned.1.call-done), dimensions={1,2} | broadcast | bytes 13369344 | tf_op jit(solution)/shard_map/stack | solution.py:39
  452.4 0.0 copy-start.2
  452.4 6.7 %all-to-all-start.1 = ((bf16[16,1536,256]{2,1,0:T(8,128)(2,1)}), bf16[16,1536,256]{2,1,0:T(8,128)(2,1)}, u32[]{:S(2)}, u32[]{:S(2)}) async-start(bf16[16,1536,256]{2,1,0:T(8,128)(2,1)} %stack.5), calls=%async_computation.1 | async-start | bytes 25165824 | tf_op jit(solution)/shard_map/all_to_all | solution.py:39
  459.1 0.0 copy-done.2
  459.1 1.3 pad_maximum_fusion
  460.4 184.0 %all-to-all-done.1 = bf16[16,1536,256]{2,1,0:T(8,128)(2,1)} async-done(((bf16[16,1536,256]{2,1,0:T(8,128)(2,1)}), bf16[16,1536,256]{2,1,0:T(8,128)(2,1)}, u32[]{:S(2)}, u32[]{:S(2)}) %all-to-all-start.1) | async-done | bytes 12582944 | tf_op jit(solution)/shard_map/all_to_all | solution.py:39
  644.4 1.2 constant_dynamic-slice_fusion
  645.6 7.3 %fusion = bf16[1536,1536]{1,0:T(8,128)(2,1)} fusion(f32[1536,1536]{1,0:T(8,128)} %copy-done, bf16[1536,256]{1,0:T(8,128)(2,1)S(1)} %copy-done.2, bf16[1536,256]{1,0:T(8,128)(2,1)S(1)} %bitcast.15), kind=kOutput, calls=%fused_computation.2 | convolution fusion | flops 1212678144 | bytes 15728640 | tf_op jit(solution)/shard_map/dot_general | solution.py:13
  (3 shorter events, 0.0 us)
Async XLA Ops:
  7.2 118.1 %all-reduce.3.cloned.1.call-start = ((), (), s32[]{:S(2)}) async-start(), calls=%async_computation.2 | async-start | bytes 1572864 | tf_op jit(solution)/shard_map/psum | solution.py:9
  132.1 193.2 %copy-start.1 = (bf16[1536,256]{1,0:T(8,128)(2,1)S(1)}, bf16[1536,256]{1,0:T(8,128)(2,1)}, u32[]{:S(2)}) copy-start(bf16[1536,256]{1,0:T(8,128)(2,1)} %all-reduce.3.cloned.1.call-done) | copy-start | bytes 2359300
  132.1 192.0 %all-to-all-start = ((bf16[16,1536,256]{2,1,0:T(8,128)(2,1)}), bf16[16,1536,256]{2,1,0:T(8,128)(2,1)}, u32[]{:S(2)}, u32[]{:S(2)}) async-start(bf16[16,1536,256]{2,1,0:T(8,128)(2,1)} %stack.4), calls=%async_computation | async-start | bytes 25165824 | tf_op jit(solution)/shard_map/all_to_all | solution.py:39
  138.8 306.8 %all-reduce.5.cloned.1.call-start = ((), (), s32[]{:S(2)}) async-start(), calls=%async_computation.3 | async-start | bytes 1572864 | tf_op jit(solution)/shard_map/psum | solution.py:9
  325.3 7.4 %copy-start.3 = (bf16[2,256,256]{2,1,0:T(8,128)(2,1)S(1)}, bf16[2,256,256]{2,1,0:T(8,128)(2,1)}, u32[]{:S(2)}) copy-start(bf16[2,256,256]{2,1,0:T(8,128)(2,1)} %param.3) | copy-start | bytes 786436
  329.1 3.6 copy-start
  452.4 6.7 %copy-start.2 = (bf16[1536,256]{1,0:T(8,128)(2,1)S(1)}, bf16[1536,256]{1,0:T(8,128)(2,1)}, u32[]{:S(2)}) copy-start(bf16[1536,256]{1,0:T(8,128)(2,1)} %all-reduce.5.cloned.1.call-done) | copy-start | bytes 2359300
  452.4 192.0 %all-to-all-start.1 = ((bf16[16,1536,256]{2,1,0:T(8,128)(2,1)}), bf16[16,1536,256]{2,1,0:T(8,128)(2,1)}, u32[]{:S(2)}, u32[]{:S(2)}) async-start(bf16[16,1536,256]{2,1,0:T(8,128)(2,1)} %stack.5), calls=%async_computation.1 | async-start | bytes 25165824 | tf_op jit(solution)/shard_map/all_to_all | solution.py:39
Sparse Core Ops, SparseCore 0:
  10.9 114.2 all-reduce.2
  334.1 111.4 all-reduce.4
